TPU v7x, 32 devices: a whole 2x2x4 slice. The times are simulated.
32 devices in a mesh: gx: 2 (over x), gy: 4 (over y, core), gz: 4 (over z).
Axes of the slice: x: 2, y: 2, z: 4, core: 2. Of those that a mesh axis runs over, the one named last changes fastest.
Arguments:
- tangent: bfloat16 [32, 8, 32, 512], P(None, 'gx', 'gy', 'gz'), may hold values from -130 to 130
- slopes: bfloat16 [32, 8, 32, 512], P(None, 'gx', 'gy', 'gz'), may hold values from -0.099609375 to 1.09375
- first_kernel: bfloat16 [27, 32, 32], replicated, may hold values from -0.21875 to 0.21875
- second_kernel: bfloat16 [27, 32, 32], replicated, may hold values from -0.21875 to 0.21875
Outputs:
- next_vector: float32 [32, 8, 32, 512], P(None, 'gx', 'gy', 'gz')
- jvp_norm: float32 [1], replicated
All inputs are finite; a program needn't handle non-finite values.
Results may differ from a plain program's by a relative error of at most 0.0038.
Values may be sent and summed in bfloat16 or wider, within the bound.
A program may use at most 192 MiB of HBM per device.

v0:
```python
import functools
import itertools

import jax
import jax.numpy as jnp
from jax import lax
from jax.experimental import pallas as pl
from jax.experimental.pallas import tpu as pltpu
from jax.sharding import PartitionSpec as P

AXES = ("gx", "gy", "gz")
MESH = pl.DeviceIdType.MESH
PAD = 16
DIRS = [d for d in itertools.product((-1, 0, 1), repeat=3) if d != (0, 0, 0)]


def kernel(
    counts, ch, t_ref, s_ref, k1t_ref, k2t_ref, k2_ref, k1_ref, out_ref, norm_ref,
    field, edge, rows, shifted, taps, weights, sums_x, sums_y, sums_z,
    send_sem, recv_sem, sum_send, sum_recv,
):
    nx, nz, lanes = t_ref.shape
    ny = lanes // ch
    wide = field.shape[3]
    me = tuple(lax.axis_index(a) for a in AXES)

    def inside(d, sign):
        ok = jnp.bool_(True)
        for m, n, s in zip(me, counts, d):
            if s * sign > 0:
                ok = jnp.logical_and(ok, m < n - 1)
            elif s * sign < 0:
                ok = jnp.logical_and(ok, m > 0)
        return ok

    def others(axis):
        n = counts[axis]
        for k in range(1, n):
            there = list(me)
            there[axis] = lax.rem(me[axis] + k, n)
            yield k, tuple(there)

    field[...] = jnp.zeros_like(field)
    rows[...] = jnp.zeros_like(rows)

    barrier = pltpu.get_barrier_semaphore()
    total = jnp.int32(0)
    for d in DIRS:
        ok = inside(d, 1)
        total = total + ok.astype(jnp.int32)

        @pl.when(ok)
        def _():
            there = tuple(m + s for m, s in zip(me, d))
            pl.semaphore_signal(barrier, inc=1, device_id=there, device_id_type=MESH)

    for axis in range(3):
        for _, there in others(axis):
            pl.semaphore_signal(barrier, inc=1, device_id=there, device_id_type=MESH)
            total = total + 1

    def copy_of(r, i):
        dx, dy, dz = DIRS[i]
        if dz == 0:
            z_from, z_to, size = PAD, PAD, nz
        elif dz > 0:
            z_from, z_to, size = nz, 0, PAD
        else:
            z_from, z_to, size = PAD, nz + PAD, PAD
        if dy == 0:
            if dx == 0:
                x_from, x_to, planes = 1, 1, nx
            elif dx > 0:
                x_from, x_to, planes = nx, 0, 1
            else:
                x_from, x_to, planes = 1, nx + 1, 1
            src = field.at[r, pl.ds(x_from, planes), pl.ds(z_from, size), pl.ds(0, lanes)]
            dst = field.at[r, pl.ds(x_to, planes), pl.ds(z_to, size), pl.ds(0, lanes)]
        else:
            src = edge.at[r, (dy + 1) // 2, pl.ds(z_from - PAD, size), :]
            dst = rows.at[r, dx + 1, (1 - dy) // 2, pl.ds(z_to, size), :]
        there = tuple(
            m if s == 0 else jnp.clip(m + s, 0, n - 1) for m, s, n in zip(me, DIRS[i], counts)
        )
        return pltpu.make_async_remote_copy(
            src_ref=src, dst_ref=dst, send_sem=send_sem.at[r, i], recv_sem=recv_sem.at[r, i],
            device_id=there, device_id_type=MESH,
        )

    def sum_copies(axis, buf):
        return [
            pltpu.make_async_remote_copy(
                src_ref=buf.at[me[axis]], dst_ref=buf.at[me[axis]],
                send_sem=sum_send.at[axis, k], recv_sem=sum_recv.at[axis, k],
                device_id=there, device_id_type=MESH,
            )
            for k, there in others(axis)
        ]

    def start_sum(axis, buf, value):
        buf[me[axis]] = value
        for copy in sum_copies(axis, buf):
            copy.start()

    def finish_sum(axis, buf):
        for copy in sum_copies(axis, buf):
            copy.wait()
        result = buf[0]
        for j in range(1, counts[axis]):
            result = result + buf[j]
        return result

    lane_block = lax.broadcasted_iota(jnp.int32, (ch, lanes), 1) // ch
    lane_inner = lax.rem(lax.broadcasted_iota(jnp.int32, (ch, lanes), 1), ch)
    tiler = (lax.broadcasted_iota(jnp.int32, (ch, lanes), 0) == lane_inner)
    tiler = tiler.astype(jnp.float32).astype(jnp.bfloat16)

    def build(k_ref, flip):
        taps[...] = jnp.dot(k_ref[...], tiler, preferred_element_type=jnp.float32)

        def group(g, carry):
            mats = []
            for b in range(3):
                tap = 9 * (g // 3) + 3 * b + g % 3
                tap = 26 - tap if flip else tap
                mats.append(taps[pl.ds(pl.multiple_of(tap * ch, ch), ch), :])
            strips = []
            for y in list(range(ny)) + [-1, ny]:
                strip = jnp.zeros((ch, lanes), jnp.float32)
                for b in range(3):
                    if 0 <= y - (b - 1) < ny:
                        strip = jnp.where(lane_block == y - (b - 1), mats[b], strip)
                strips.append(strip)
            strips.append(jnp.zeros((wide - (ny + 2) * ch, lanes), jnp.float32))
            tile = jnp.concatenate(strips, axis=0).astype(jnp.bfloat16)
            weights[pl.ds(pl.multiple_of(g * wide, wide), wide), :] = tile
            return carry

        lax.fori_loop(0, 9, group, 0)

    def conv(r, value, k_ref, flip):
        value = value.reshape(nx, nz, lanes)
        field[r, 1 : nx + 1, PAD : PAD + nz, 0:lanes] = value
        for s in range(2):
            low = s * (ny - 1) * ch
            for x in range(nx):
                edge[r, s, :, x * ch : (x + 1) * ch] = value[x, :, low : low + ch]
        if r == 0:
            pl.semaphore_wait(barrier, total)
        for i, d in enumerate(DIRS):
            @pl.when(inside(d, 1))
            def _():
                copy_of(r, i).start()
        build(k_ref, flip)
        for i, d in enumerate(DIRS):
            @pl.when(inside(d, -1))
            def _():
                copy_of(r, i).wait_recv()
        for s in range(2):
            low = lanes + s * ch
            field[r, 0, :, low : low + ch] = rows[r, 2, s, :, (nx - 1) * ch : nx * ch]
            for x in range(nx):
                field[r, 1 + x, :, low : low + ch] = rows[r, 1, s, :, x * ch : (x + 1) * ch]
            field[r, nx + 1, :, low : low + ch] = rows[r, 0, s, :, 0:ch]
        for c in range(3):
            shifted[c] = field[r, :, PAD - 1 + c : PAD - 1 + c + nz, :]
        pieces = [
            shifted[c, a : a + nx].reshape(nx * nz, wide) for a in range(3) for c in range(3)
        ]
        stacked = jnp.concatenate(pieces, axis=1)
        return jnp.dot(stacked, weights[...], preferred_element_type=jnp.float32)

    slopes = s_ref[...].reshape(nx * nz, lanes).astype(jnp.float32)
    inner = conv(0, t_ref[...], k1t_ref, False)
    hidden = (slopes * inner).astype(jnp.bfloat16)
    image = conv(1, hidden, k2t_ref, False)
    squares = image * image
    squares = squares[:, 0:128] + squares[:, 128:256]
    start_sum(0, sums_x, jnp.sum(squares.reshape(nx * nz // 8, 8, 128), axis=0))
    back = conv(2, image.astype(jnp.bfloat16), k2_ref, True)
    start_sum(1, sums_y, finish_sum(0, sums_x))
    slopes = s_ref[...].reshape(nx * nz, lanes).astype(jnp.float32)
    pulled = (slopes * back).astype(jnp.bfloat16)
    result = conv(3, pulled, k1_ref, True)
    start_sum(2, sums_z, finish_sum(1, sums_y))
    out_ref[...] = result.reshape(nx, nz, lanes)
    norm = jnp.sqrt(jnp.sum(finish_sum(2, sums_z), keepdims=True) + 1e-06)
    norm_ref[...] = norm
    out_ref[...] = out_ref[...] / norm.reshape(1, 1, 1)

    for r in range(4):
        for i, d in enumerate(DIRS):
            @pl.when(inside(d, 1))
            def _():
                copy_of(r, i).wait_send()


def on_device(counts, tangent, slopes, first_kernel, second_kernel):
    ch, nx, ny, nz = tangent.shape
    lanes = ny * ch
    wide = lanes + 128

    def spread(array):
        return jnp.transpose(array, (1, 3, 2, 0)).reshape(nx, nz, lanes)

    def flat(array):
        return array.reshape(-1, ch)

    first_t = jnp.swapaxes(first_kernel, 1, 2)
    second_t = jnp.swapaxes(second_kernel, 1, 2)
    most = max(counts)
    result, norm = pl.pallas_call(
        functools.partial(kernel, counts, ch),
        out_shape=(
            jax.ShapeDtypeStruct((nx, nz, lanes), jnp.float32),
            jax.ShapeDtypeStruct((1, 1), jnp.float32),
        ),
        in_specs=[pl.BlockSpec(memory_space=pltpu.VMEM)] * 6,
        out_specs=(pl.BlockSpec(memory_space=pltpu.VMEM),) * 2,
        scratch_shapes=[
            pltpu.VMEM((4, nx + 2, nz + 2 * PAD, wide), jnp.bfloat16),
            pltpu.VMEM((4, 2, nz, nx * ch), jnp.bfloat16),
            pltpu.VMEM((4, 3, 2, nz + 2 * PAD, nx * ch), jnp.bfloat16),
            pltpu.VMEM((3, nx + 2, nz, wide), jnp.bfloat16),
            pltpu.VMEM((27 * ch, lanes), jnp.float32),
            pltpu.VMEM((9 * wide, lanes), jnp.bfloat16),
            pltpu.VMEM((counts[0], 8, 128), jnp.float32),
            pltpu.VMEM((counts[1], 8, 128), jnp.float32),
            pltpu.VMEM((counts[2], 8, 128), jnp.float32),
            pltpu.SemaphoreType.DMA((4, len(DIRS))),
            pltpu.SemaphoreType.DMA((4, len(DIRS))),
            pltpu.SemaphoreType.DMA((3, most)),
            pltpu.SemaphoreType.DMA((3, most)),
        ],
        compiler_params=pltpu.CompilerParams(
            collective_id=0, has_side_effects=True, vmem_limit_bytes=48 * 1024 * 1024
        ),
        name="denoiser_step",
    )(spread(tangent), spread(slopes), flat(first_t), flat(second_t), flat(second_kernel), flat(first_kernel))
    result = result.reshape(nx, nz, ny, ch)
    return (jnp.transpose(result, (3, 0, 2, 1)), norm.reshape(1))


def solution(mesh):
    counts = tuple(mesh.shape[a] for a in AXES)
    return jax.shard_map(
        functools.partial(on_device, counts),
        mesh=mesh,
        in_specs=(P(None, "gx", "gy", "gz"), P(None, "gx", "gy", "gz"), P(), P()),
        out_specs=(P(None, "gx", "gy", "gz"), P()),
        check_vma=False,
    )
```

profile of v0, /device:TPU:0, one launch (start us, length us, event | category | flops | bytes accessed | tf_op | source)
XLA Modules:
  0.0 46.2 jit_solution(1666929641013767530)
XLA Ops:
  0.6 0.0 copy-start
  0.6 1.1 %copy.14 = bf16[27,32,32]{2,1,0:T(8,128)(2,1)S(1)} copy(bf16[27,32,32]{1,2,0:T(8,128)(2,1)} %bitcast.18) | data formatting | bytes 110592 | tf_op jit(solution)/shard_map/transpose | solution.py:210
  1.8 0.0 copy-start.2
  1.8 0.0 copy-done
  1.8 0.2 copy.13
  2.0 0.8 %copy-done.2 = bf16[32,4,8,128]{3,2,1,0:T(8,128)(2,1)S(1)} copy-done((bf16[32,4,8,128]{3,2,1,0:T(8,128)(2,1)S(1)}, bf16[32,4,8,128]{3,2,1,0:T(8,128)(2,1)}, u32[]{:S(2)}) %copy-start.2) | copy-done | bytes 262168
  2.7 0.1 copy.11
  2.8 0.0 copy-start.3
  2.8 0.1 copy.15.t_ref
  3.0 0.8 %copy-done.3 = bf16[32,4,8,128]{3,2,1,0:T(8,128)(2,1)S(1)} copy-done((bf16[32,4,8,128]{3,2,1,0:T(8,128)(2,1)S(1)}, bf16[32,4,8,128]{3,2,1,0:T(8,128)(2,1)}, u32[]{:S(2)}) %copy-start.3) | copy-done | bytes 262168
  3.8 0.1 copy.12
  3.9 0.0 copy-start.1
  3.9 0.1 copy.16.s_ref
  4.1 0.8 %copy-done.1 = bf16[27,32,32]{2,1,0:T(8,128)(2,1)S(1)} copy-done((bf16[27,32,32]{2,1,0:T(8,128)(2,1)S(1)}, bf16[27,32,32]{2,1,0:T(8,128)(2,1)}, u32[]{:S(2)}) %copy-start.1) | copy-done | bytes 55320
  4.8 38.3 %denoiser_step.1 = (f32[4,128,256]{2,1,0:T(8,128)S(1)}, f32[1,1]{1,0:T(1,128)}) custom-call(bf16[4,128,256]{2,1,0:T(8,128)(2,1)S(1)} %copy.15.t_ref, bf16[4,128,256]{2,1,0:T(8,128)(2,1)S(1)} %copy.16.s_ref, bf16[864,32]{1,0:T(8,128)(2,1)S(1)} %bitcast.21, bf16[864,32]{1,0:T(8,128)(2,1)S(1)} %bitcast.20, bf16[864,32]{1,0:T(8,128)(2,1)S(1)} %bitcast.19, ...), custom_call_target="tpu_custom_call" | custom-call | tf_op jit(solution)/shard_map/denoiser_step/pallas_call | solution.py:212
  43.2 0.2 copy.17
  43.4 1.1 %copy.18 = f32[32,4,8,128]{3,2,1,0:T(8,128)} copy(f32[32,4,8,128]{3,0,2,1:T(8,128)S(1)} %bitcast.22) | data formatting | bytes 1048576
Async XLA Ops:
  0.6 1.2 %copy-start = (bf16[27,32,32]{2,1,0:T(8,128)(2,1)S(1)}, bf16[27,32,32]{2,1,0:T(8,128)(2,1)}, u32[]{:S(2)}) copy-start(bf16[27,32,32]{2,1,0:T(8,128)(2,1)} %param.6) | copy-start | bytes 165892
  1.8 1.0 %copy-start.2 = (bf16[32,4,8,128]{3,2,1,0:T(8,128)(2,1)S(1)}, bf16[32,4,8,128]{3,2,1,0:T(8,128)(2,1)}, u32[]{:S(2)}) copy-start(bf16[32,4,8,128]{3,2,1,0:T(8,128)(2,1)} %param.4) | copy-start | bytes 786436
  2.8 1.0 %copy-start.3 = (bf16[32,4,8,128]{3,2,1,0:T(8,128)(2,1)S(1)}, bf16[32,4,8,128]{3,2,1,0:T(8,128)(2,1)}, u32[]{:S(2)}) copy-start(bf16[32,4,8,128]{3,2,1,0:T(8,128)(2,1)} %param.5) | copy-start | bytes 786436
  3.9 0.9 %copy-start.1 = (bf16[27,32,32]{2,1,0:T(8,128)(2,1)S(1)}, bf16[27,32,32]{2,1,0:T(8,128)(2,1)}, u32[]{:S(2)}) copy-start(bf16[27,32,32]{2,1,0:T(8,128)(2,1)} %param.7) | copy-start | bytes 165892
where the time goes:
time: 46.5 us; the launch traced here: 46.2 us
  Pallas kernels  38.3 us (82%)
  local copies, waits for them, and re-layouts  5.43 us (12%)
  between operations  2.46 us (5%)
    pallas_call x1, Pallas kernels, on_device(): pl.pallas_call(functools.partial(kernel, counts, ch), out_shape=(jax.Shap...  38.3 us
    unnamed x11, local copies, waits for them, and re-layouts  3.67 us
    transpose x1, local copies, waits for them, and re-layouts, on_device(): second_t = jnp.swapaxes(second_kernel, 1, 2)  1.13 us

commit v1 on v0

--- a/solution.py
+++ b/solution.py
@@ -11,12 +11,15 @@
 AXES = ("gx", "gy", "gz")
 MESH = pl.DeviceIdType.MESH
 PAD = 16
-DIRS = [d for d in itertools.product((-1, 0, 1), repeat=3) if d != (0, 0, 0)]
+DIRS = sorted(
+    (d for d in itertools.product((-1, 0, 1), repeat=3) if d != (0, 0, 0)),
+    key=lambda d: (d[1:] != (0, 0), sum(map(abs, d)), abs(d[0])),
+)
 
 
 def kernel(
     counts, ch, t_ref, s_ref, k1t_ref, k2t_ref, k2_ref, k1_ref, out_ref, norm_ref,
-    field, edge, rows, shifted, taps, weights, sums_x, sums_y, sums_z,
+    field, edge, edge_x, rows, rows_x, shifted, shifted_x, acc, taps, weights, sums_x, sums_y, sums_z,
     send_sem, recv_sem, sum_send, sum_recv,
 ):
     nx, nz, lanes = t_ref.shape
@@ -42,6 +45,8 @@
 
     field[...] = jnp.zeros_like(field)
     rows[...] = jnp.zeros_like(rows)
+    rows_x[...] = jnp.zeros_like(rows_x)
+    shifted[...] = jnp.zeros_like(shifted)
 
     barrier = pltpu.get_barrier_semaphore()
     total = jnp.int32(0)
@@ -76,6 +81,9 @@
                 x_from, x_to, planes = 1, nx + 1, 1
             src = field.at[r, pl.ds(x_from, planes), pl.ds(z_from, size), pl.ds(0, lanes)]
             dst = field.at[r, pl.ds(x_to, planes), pl.ds(z_to, size), pl.ds(0, lanes)]
+        elif dx != 0 and dz == 0:
+            src = edge_x.at[r, (dx + 1) // 2, (dy + 1) // 2]
+            dst = rows_x.at[r, (dx + 1) // 2, (1 - dy) // 2]
         else:
             src = edge.at[r, (dy + 1) // 2, pl.ds(z_from - PAD, size), :]
             dst = rows.at[r, dx + 1, (1 - dy) // 2, pl.ds(z_to, size), :]
@@ -141,10 +149,17 @@
     def conv(r, value, k_ref, flip):
         value = value.reshape(nx, nz, lanes)
         field[r, 1 : nx + 1, PAD : PAD + nz, 0:lanes] = value
+        parts = 128 // ch
+        quarter = nz // parts
         for s in range(2):
             low = s * (ny - 1) * ch
             for x in range(nx):
                 edge[r, s, :, x * ch : (x + 1) * ch] = value[x, :, low : low + ch]
+            for side, x in enumerate((0, nx - 1)):
+                for q in range(parts):
+                    edge_x[r, side, s, :, q * ch : (q + 1) * ch] = value[
+                        x, q * quarter : (q + 1) * quarter, low : low + ch
+                    ]
         if r == 0:
             pl.semaphore_wait(barrier, total)
         for i, d in enumerate(DIRS):
@@ -152,23 +167,52 @@
             def _():
                 copy_of(r, i).start()
         build(k_ref, flip)
-        for i, d in enumerate(DIRS):
-            @pl.when(inside(d, -1))
-            def _():
-                copy_of(r, i).wait_recv()
+        def arrive(along_x):
+            for i, d in enumerate(DIRS):
+                if (d[0] != 0) == along_x:
+                    @pl.when(inside(d, -1))
+                    def _():
+                        copy_of(r, i).wait_recv()
+
+        arrive(False)
         for s in range(2):
             low = lanes + s * ch
-            field[r, 0, :, low : low + ch] = rows[r, 2, s, :, (nx - 1) * ch : nx * ch]
             for x in range(nx):
                 field[r, 1 + x, :, low : low + ch] = rows[r, 1, s, :, x * ch : (x + 1) * ch]
-            field[r, nx + 1, :, low : low + ch] = rows[r, 0, s, :, 0:ch]
         for c in range(3):
-            shifted[c] = field[r, :, PAD - 1 + c : PAD - 1 + c + nz, :]
+            shifted[c, 1 : nx + 1] = field[r, 1 : nx + 1, PAD - 1 + c : PAD - 1 + c + nz, :]
         pieces = [
             shifted[c, a : a + nx].reshape(nx * nz, wide) for a in range(3) for c in range(3)
         ]
         stacked = jnp.concatenate(pieces, axis=1)
-        return jnp.dot(stacked, weights[...], preferred_element_type=jnp.float32)
+        acc[...] = jnp.dot(stacked, weights[...], preferred_element_type=jnp.float32)
+        if r == 2:
+            start_sum(1, sums_y, finish_sum(0, sums_x))
+        arrive(True)
+        for side, plane, out, a in ((1, 0, 0, 0), (0, nx + 1, nx - 1, 2)):
+            @pl.when(inside((2 * side - 1, 0, 0), -1))
+            def _():
+                x = nx - 1 if side else 0
+                for s in range(2):
+                    low = lanes + s * ch
+                    for z in (0, nz + PAD):
+                        field[r, plane, z : z + PAD, low : low + ch] = rows[
+                            r, 2 * side, s, z : z + PAD, x * ch : (x + 1) * ch
+                        ]
+                    for q in range(parts):
+                        z = PAD + q * quarter
+                        field[r, plane, z : z + quarter, low : low + ch] = rows_x[
+                            r, side, s, :, q * ch : (q + 1) * ch
+                        ]
+                for c in range(3):
+                    shifted_x[c] = field[r, plane, PAD - 1 + c : PAD - 1 + c + nz, :]
+                more = jnp.dot(
+                    jnp.concatenate([shifted_x[c] for c in range(3)], axis=1),
+                    weights[3 * a * wide : 3 * (a + 1) * wide, :],
+                    preferred_element_type=jnp.float32,
+                )
+                acc[out * nz : (out + 1) * nz, :] += more
+        return acc[...]
 
     slopes = s_ref[...].reshape(nx * nz, lanes).astype(jnp.float32)
     inner = conv(0, t_ref[...], k1t_ref, False)
@@ -178,15 +222,13 @@
     squares = squares[:, 0:128] + squares[:, 128:256]
     start_sum(0, sums_x, jnp.sum(squares.reshape(nx * nz // 8, 8, 128), axis=0))
     back = conv(2, image.astype(jnp.bfloat16), k2_ref, True)
-    start_sum(1, sums_y, finish_sum(0, sums_x))
+    start_sum(2, sums_z, finish_sum(1, sums_y))
     slopes = s_ref[...].reshape(nx * nz, lanes).astype(jnp.float32)
     pulled = (slopes * back).astype(jnp.bfloat16)
     result = conv(3, pulled, k1_ref, True)
-    start_sum(2, sums_z, finish_sum(1, sums_y))
-    out_ref[...] = result.reshape(nx, nz, lanes)
     norm = jnp.sqrt(jnp.sum(finish_sum(2, sums_z), keepdims=True) + 1e-06)
     norm_ref[...] = norm
-    out_ref[...] = out_ref[...] / norm.reshape(1, 1, 1)
+    out_ref[...] = (result / norm).reshape(nx, nz, lanes)
 
     for r in range(4):
         for i, d in enumerate(DIRS):
@@ -220,8 +262,12 @@
         scratch_shapes=[
             pltpu.VMEM((4, nx + 2, nz + 2 * PAD, wide), jnp.bfloat16),
             pltpu.VMEM((4, 2, nz, nx * ch), jnp.bfloat16),
+            pltpu.VMEM((4, 2, 2, nz * ch // 128, 128), jnp.bfloat16),
             pltpu.VMEM((4, 3, 2, nz + 2 * PAD, nx * ch), jnp.bfloat16),
+            pltpu.VMEM((4, 2, 2, nz * ch // 128, 128), jnp.bfloat16),
             pltpu.VMEM((3, nx + 2, nz, wide), jnp.bfloat16),
+            pltpu.VMEM((3, nz, wide), jnp.bfloat16),
+            pltpu.VMEM((nx * nz, lanes), jnp.float32),
             pltpu.VMEM((27 * ch, lanes), jnp.float32),
             pltpu.VMEM((9 * wide, lanes), jnp.bfloat16),
             pltpu.VMEM((counts[0], 8, 128), jnp.float32),

time: 46.5 us -> 40.3 us (0.87)
  Pallas kernels: 38.3 us -> 32.2 us
    pallas_call x1, Pallas kernels: 38.3 us -> 32.2 us  [on_device(): pl.pallas_call(functools.partial(kernel, counts, ch), out_shape=(jax.Shap...]
where the time goes in v1:
time: 40.3 us; the launch traced here: 40.1 us
  Pallas kernels  32.2 us (80%)
  local copies, waits for them, and re-layouts  5.43 us (13%)
  between operations  2.46 us (6%)
    pallas_call x1, Pallas kernels, on_device(): pl.pallas_call(functools.partial(kernel, counts, ch), out_shape=(jax.Shap...  32.2 us
    unnamed x11, local copies, waits for them, and re-layouts  3.67 us
    transpose x1, local copies, waits for them, and re-layouts, on_device(): second_t = jnp.swapaxes(second_kernel, 1, 2)  1.13 us

profile of v1, /device:TPU:0, one launch (start us, length us, event | category | flops | bytes accessed | tf_op | source)
XLA Modules:
  0.0 40.1 jit_solution(3002440150895397679)
XLA Ops:
  0.6 0.0 copy-start
  0.6 1.1 %copy.14 = bf16[27,32,32]{2,1,0:T(8,128)(2,1)S(1)} copy(bf16[27,32,32]{1,2,0:T(8,128)(2,1)} %bitcast.18) | data formatting | bytes 110592 | tf_op jit(solution)/shard_map/transpose | solution.py:252
  1.8 0.0 copy-start.2
  1.8 0.0 copy-done
  1.8 0.2 copy.13
  2.0 0.8 %copy-done.2 = bf16[32,4,8,128]{3,2,1,0:T(8,128)(2,1)S(1)} copy-done((bf16[32,4,8,128]{3,2,1,0:T(8,128)(2,1)S(1)}, bf16[32,4,8,128]{3,2,1,0:T(8,128)(2,1)}, u32[]{:S(2)}) %copy-start.2) | copy-done | bytes 262168
  2.7 0.1 copy.11
  2.8 0.0 copy-start.3
  2.8 0.1 copy.15.t_ref
  3.0 0.8 %copy-done.3 = bf16[32,4,8,128]{3,2,1,0:T(8,128)(2,1)S(1)} copy-done((bf16[32,4,8,128]{3,2,1,0:T(8,128)(2,1)S(1)}, bf16[32,4,8,128]{3,2,1,0:T(8,128)(2,1)}, u32[]{:S(2)}) %copy-start.3) | copy-done | bytes 262168
  3.8 0.1 copy.12
  3.9 0.0 copy-start.1
  3.9 0.1 copy.16.s_ref
  4.1 0.8 %copy-done.1 = bf16[27,32,32]{2,1,0:T(8,128)(2,1)S(1)} copy-done((bf16[27,32,32]{2,1,0:T(8,128)(2,1)S(1)}, bf16[27,32,32]{2,1,0:T(8,128)(2,1)}, u32[]{:S(2)}) %copy-start.1) | copy-done | bytes 55320
  4.8 32.2 %denoiser_step.1 = (f32[4,128,256]{2,1,0:T(8,128)S(1)}, f32[1,1]{1,0:T(1,128)}) custom-call(bf16[4,128,256]{2,1,0:T(8,128)(2,1)S(1)} %copy.15.t_ref, bf16[4,128,256]{2,1,0:T(8,128)(2,1)S(1)} %copy.16.s_ref, bf16[864,32]{1,0:T(8,128)(2,1)S(1)} %bitcast.21, bf16[864,32]{1,0:T(8,128)(2,1)S(1)} %bitcast.20, bf16[864,32]{1,0:T(8,128)(2,1)S(1)} %bitcast.19, ...), custom_call_target="tpu_custom_call" | custom-call | tf_op jit(solution)/shard_map/denoiser_step/pallas_call | solution.py:254
  37.0 0.2 copy.17
  37.2 1.1 %copy.18 = f32[32,4,8,128]{3,2,1,0:T(8,128)} copy(f32[32,4,8,128]{3,0,2,1:T(8,128)S(1)} %bitcast.22) | data formatting | bytes 1048576
Async XLA Ops:
  0.6 1.2 %copy-start = (bf16[27,32,32]{2,1,0:T(8,128)(2,1)S(1)}, bf16[27,32,32]{2,1,0:T(8,128)(2,1)}, u32[]{:S(2)}) copy-start(bf16[27,32,32]{2,1,0:T(8,128)(2,1)} %param.6) | copy-start | bytes 165892
  1.8 1.0 %copy-start.2 = (bf16[32,4,8,128]{3,2,1,0:T(8,128)(2,1)S(1)}, bf16[32,4,8,128]{3,2,1,0:T(8,128)(2,1)}, u32[]{:S(2)}) copy-start(bf16[32,4,8,128]{3,2,1,0:T(8,128)(2,1)} %param.4) | copy-start | bytes 786436
  2.8 1.0 %copy-start.3 = (bf16[32,4,8,128]{3,2,1,0:T(8,128)(2,1)S(1)}, bf16[32,4,8,128]{3,2,1,0:T(8,128)(2,1)}, u32[]{:S(2)}) copy-start(bf16[32,4,8,128]{3,2,1,0:T(8,128)(2,1)} %param.5) | copy-start | bytes 786436
  3.9 0.9 %copy-start.1 = (bf16[27,32,32]{2,1,0:T(8,128)(2,1)S(1)}, bf16[27,32,32]{2,1,0:T(8,128)(2,1)}, u32[]{:S(2)}) copy-start(bf16[27,32,32]{2,1,0:T(8,128)(2,1)} %param.7) | copy-start | bytes 165892

commit v2 on v1

v2 whole, which is shorter than its diff:
```python
import functools
import itertools

import jax
import jax.numpy as jnp
from jax import lax
from jax.experimental import pallas as pl
from jax.experimental.pallas import tpu as pltpu
from jax.sharding import PartitionSpec as P

AXES = ("gx", "gy", "gz")
MESH = pl.DeviceIdType.MESH
PAD = 16
DIRS = sorted(
    (d for d in itertools.product((-1, 0, 1), repeat=3) if d != (0, 0, 0)),
    key=lambda d: (d[1:] != (0, 0), sum(map(abs, d)), abs(d[0])),
)


def kernel(
    counts, ch, t_ref, s_ref, k1t_ref, k2t_ref, k2_ref, k1_ref, out_ref, norm_ref,
    field, slopes, edge, edge_x, rows, rows_x, line,
    shifted, shifted_y, shifted_x, acc, taps, weights, sums_x, sums_y, sums_z,
    send_sem, recv_sem, slope_send, slope_recv, sum_send, sum_recv,
):
    nx, nz, lanes = t_ref.shape
    ny = lanes // ch
    ext = nz + 2 * PAD
    own = 2 * PAD
    parts = 128 // ch
    per_a = 4 * lanes
    me = tuple(lax.axis_index(a) for a in AXES)

    def inside(d, sign):
        ok = jnp.bool_(True)
        for m, n, s in zip(me, counts, d):
            if s * sign > 0:
                ok = jnp.logical_and(ok, m < n - 1)
            elif s * sign < 0:
                ok = jnp.logical_and(ok, m > 0)
        return ok

    def others(axis):
        n = counts[axis]
        for k in range(1, n):
            there = list(me)
            there[axis] = lax.rem(me[axis] + k, n)
            yield k, tuple(there)

    for buf in (field, slopes, rows, rows_x, line, shifted, shifted_y, shifted_x, weights):
        buf[...] = jnp.zeros_like(buf)

    barrier = pltpu.get_barrier_semaphore()
    total = jnp.int32(0)
    for d in DIRS:
        ok = inside(d, 1)
        total = total + ok.astype(jnp.int32)

        @pl.when(ok)
        def _():
            there = tuple(m + s for m, s in zip(me, d))
            pl.semaphore_signal(barrier, inc=1, device_id=there, device_id_type=MESH)

    for axis in range(3):
        for _, there in others(axis):
            pl.semaphore_signal(barrier, inc=1, device_id=there, device_id_type=MESH)
            total = total + 1

    def remote(src, dst, send, recv, d):
        there = tuple(
            m if s == 0 else jnp.clip(m + s, 0, n - 1) for m, s, n in zip(me, d, counts)
        )
        return pltpu.make_async_remote_copy(
            src_ref=src, dst_ref=dst, send_sem=send, recv_sem=recv,
            device_id=there, device_id_type=MESH,
        )

    def copy_of(r, i):
        dx, dy, dz = DIRS[i]
        if dz == 0:
            z_from, z_to, size = (own, own, nz) if r == 0 else (PAD, PAD, ext)
        elif dz > 0:
            z_from, z_to, size = own + nz - PAD, PAD, PAD
        else:
            z_from, z_to, size = own, own + nz, PAD
        if dy == 0:
            if dx == 0:
                x_from, x_to, planes = 1, 1, nx
            elif dx > 0:
                x_from, x_to, planes = nx, 0, 1
            else:
                x_from, x_to, planes = 1, nx + 1, 1
            src = field.at[r, pl.ds(x_from, planes), pl.ds(z_from, size), :]
            dst = field.at[r, pl.ds(x_to, planes), pl.ds(z_to, size), :]
        elif dx != 0 and dz == 0:
            size = (nz if r == 0 else nz + 4 * PAD) // parts
            src = edge_x.at[r, (dx + 1) // 2, (dy + 1) // 2, pl.ds(0, size), :]
            dst = rows_x.at[r, (dx + 1) // 2, (1 - dy) // 2, pl.ds(0, size), :]
        else:
            src = edge.at[r, (dy + 1) // 2, pl.ds(z_from, size), :]
            dst = rows.at[r, dx + 1, (1 - dy) // 2, pl.ds(z_to, size), :]
        return remote(src, dst, send_sem.at[r, i], recv_sem.at[r, i], DIRS[i])

    def dirs_of(r):
        return [(i, d) for i, d in enumerate(DIRS) if r == 0 or d[2] == 0]

    def slope_copy(side):
        z_from, z_to = (nz, 0) if side else (PAD, nz + PAD)
        return remote(
            slopes.at[:, pl.ds(z_from, PAD), :], slopes.at[:, pl.ds(z_to, PAD), :],
            slope_send.at[side], slope_recv.at[side], (0, 0, 2 * side - 1),
        )

    def sum_copies(axis, buf):
        return [
            pltpu.make_async_remote_copy(
                src_ref=buf.at[me[axis]], dst_ref=buf.at[me[axis]],
                send_sem=sum_send.at[axis, k], recv_sem=sum_recv.at[axis, k],
                device_id=there, device_id_type=MESH,
            )
            for k, there in others(axis)
        ]

    def start_sum(axis, buf, value):
        buf[me[axis]] = value
        for copy in sum_copies(axis, buf):
            copy.start()

    def finish_sum(axis, buf):
        for copy in sum_copies(axis, buf):
            copy.wait()
        result = buf[0]
        for j in range(1, counts[axis]):
            result = result + buf[j]
        return result

    lane_block = lax.broadcasted_iota(jnp.int32, (ch, lanes), 1) // ch
    lane_inner = lax.rem(lax.broadcasted_iota(jnp.int32, (ch, lanes), 1), ch)
    tiler = (lax.broadcasted_iota(jnp.int32, (ch, lanes), 0) == lane_inner)
    tiler = tiler.astype(jnp.float32).astype(jnp.bfloat16)

    def build(r):
        k_ref, flip = ((k1t_ref, 0), (k2t_ref, 0), (k2_ref, 1), (k1_ref, 1))[r]
        taps[...] = jnp.dot(k_ref[...], tiler, preferred_element_type=jnp.float32)

        def group(g, carry):
            mats = []
            for b in range(3):
                tap = 9 * (g // 3) + 3 * b + g % 3
                tap = 26 - tap if flip else tap
                mats.append(taps[pl.ds(pl.multiple_of(tap * ch, ch), ch), :])
            strips = []
            for y in list(range(ny)) + [-1, ny]:
                strip = jnp.zeros((ch, lanes), jnp.float32)
                for b in range(3):
                    if 0 <= y - (b - 1) < ny:
                        strip = jnp.where(lane_block == y - (b - 1), mats[b], strip)
                strips.append(strip)
            base = per_a * (g // 3)
            at = pl.multiple_of(base + lanes * (g % 3), ch)
            main = jnp.concatenate(strips[:ny], axis=0)
            weights[r % 2, pl.ds(at, lanes), :] = main.astype(jnp.bfloat16)
            at = pl.multiple_of(base + 3 * lanes + 2 * ch * (g % 3), ch)
            outer = jnp.concatenate(strips[ny:], axis=0)
            weights[r % 2, pl.ds(at, 2 * ch), :] = outer.astype(jnp.bfloat16)
            return carry

        lax.fori_loop(0, 9, group, 0)

    def conv(r):
        z, size = (own, nz) if r == 0 else (PAD, ext)
        for s in range(2):
            low = s * (ny - 1) * ch
            for x in range(nx):
                edge[r, s, z : z + size, x * ch : (x + 1) * ch] = field[
                    r, 1 + x, z : z + size, low : low + ch
                ]
        start, piece = (own, nz // parts) if r == 0 else (0, (nz + 4 * PAD) // parts)
        for s in range(2):
            low = s * (ny - 1) * ch
            for side, x in enumerate((0, nx - 1)):
                for q in range(parts):
                    z = start + q * piece
                    edge_x[r, side, s, 0:piece, q * ch : (q + 1) * ch] = field[
                        r, 1 + x, z : z + piece, low : low + ch
                    ]
        if r == 0:
            build(0)
            pl.semaphore_wait(barrier, total)
        for i, d in dirs_of(r):
            @pl.when(inside(d, 1))
            def _():
                copy_of(r, i).start()

        def arrive(keep):
            for i, d in dirs_of(r):
                if keep(d):
                    @pl.when(inside(d, -1))
                    def _():
                        copy_of(r, i).wait_recv()

        if r == 0:
            for side in range(2):
                @pl.when(inside((0, 0, 2 * side - 1), 1))
                def _():
                    slope_copy(side).start()

        arrive(lambda d: d[0] == 0 and d[1] == 0)
        lo, size = (PAD, nz) if r == 3 else (0, ext)
        for c in range(3):
            z = PAD - 1 + c + lo
            shifted[c, 1 : nx + 1, lo : lo + size, :] = field[r, 1 : nx + 1, z : z + size, :]

        def weight_rows(first, count):
            return jnp.concatenate(
                [weights[r % 2, a * per_a + first : a * per_a + first + count, :] for a in range(3)],
                axis=0,
            )

        pieces = [
            shifted[c, a : a + nx, lo : lo + size, :].reshape(nx * size, lanes)
            for a in range(3) for c in range(3)
        ]
        acc[0 : nx * size, :] = jnp.dot(
            jnp.concatenate(pieces, axis=1), weight_rows(0, 3 * lanes),
            preferred_element_type=jnp.float32,
        )
        if r < 3:
            build(r + 1)
        arrive(lambda d: d[0] == 0 and d[1] != 0)
        for c in range(3):
            z = PAD - 1 + c + lo
            for s in range(2):
                low = (2 * c + s) * ch
                for x in range(nx):
                    shifted_y[1 + x, lo : lo + size, low : low + ch] = rows[
                        r, 1, s, z : z + size, x * ch : (x + 1) * ch
                    ]
        pieces = [
            shifted_y[a : a + nx, lo : lo + size, :].reshape(nx * size, lanes) for a in range(3)
        ]
        acc[0 : nx * size, :] += jnp.dot(
            jnp.concatenate(pieces, axis=1), weight_rows(3 * lanes, lanes),
            preferred_element_type=jnp.float32,
        )
        if r == 2:
            start_sum(1, sums_y, finish_sum(0, sums_x))
        arrive(lambda d: d[0] != 0)
        for side, plane, out, a in ((1, 0, 0, 0), (0, nx + 1, nx - 1, 2)):
            @pl.when(inside((2 * side - 1, 0, 0), -1))
            def _():
                x = nx - 1 if side else 0
                for s in range(2):
                    if r == 0:
                        for z in (PAD, own + nz):
                            line[s, z : z + PAD, 0:ch] = rows[
                                r, 2 * side, s, z : z + PAD, x * ch : (x + 1) * ch
                            ]
                    for q in range(parts):
                        z = start + q * piece
                        line[s, z : z + piece, 0:ch] = rows_x[
                            r, side, s, 0:piece, q * ch : (q + 1) * ch
                        ]
                for c in range(3):
                    z = PAD - 1 + c + lo
                    shifted_x[lo : lo + size, c * lanes : (c + 1) * lanes] = field[
                        r, plane, z : z + size, :
                    ]
                    for s in range(2):
                        low = 3 * lanes + (2 * c + s) * ch
                        shifted_x[lo : lo + size, low : low + ch] = line[s, z : z + size, 0:ch]
                acc[out * size : (out + 1) * size, :] += jnp.dot(
                    shifted_x[lo : lo + size, :], weights[r % 2, a * per_a : (a + 1) * per_a, :],
                    preferred_element_type=jnp.float32,
                )
        return acc[0 : nx * size, :].reshape(nx, size, lanes)

    slopes[:, PAD : PAD + nz, :] = s_ref[...]
    field[0, 1 : nx + 1, own : own + nz, :] = t_ref[...]
    inner = conv(0)
    for side in range(2):
        @pl.when(inside((0, 0, 2 * side - 1), -1))
        def _():
            slope_copy(side).wait_recv()
    hidden = slopes[...].astype(jnp.float32) * inner
    field[1, 1 : nx + 1, PAD : PAD + ext, :] = hidden.astype(jnp.bfloat16)
    image = conv(1)
    row = lax.broadcasted_iota(jnp.int32, (1, ext, lanes), 1)
    first = jnp.where(me[2] == 0, PAD, 0)
    last = jnp.where(me[2] == counts[2] - 1, PAD + nz, ext)
    low_image = jnp.where(jnp.logical_and(row >= first, row < last), image, 0.0)
    field[2, 1 : nx + 1, PAD : PAD + ext, :] = low_image.astype(jnp.bfloat16)
    part = image[:, PAD : PAD + nz, :].reshape(nx * nz // 8, 8, lanes)
    squares = jnp.sum(part * part, axis=0)
    start_sum(0, sums_x, sum(squares[:, j : j + 128] for j in range(0, lanes, 128)))
    back = conv(2)
    start_sum(2, sums_z, finish_sum(1, sums_y))
    pulled = slopes[...].astype(jnp.float32) * back
    field[3, 1 : nx + 1, PAD : PAD + ext, :] = pulled.astype(jnp.bfloat16)
    result = conv(3)
    norm = jnp.sqrt(jnp.sum(finish_sum(2, sums_z), keepdims=True) + 1e-06)
    norm_ref[...] = norm
    out_ref[...] = result / norm.reshape(1, 1, 1)

    for r in range(4):
        for i, d in dirs_of(r):
            @pl.when(inside(d, 1))
            def _():
                copy_of(r, i).wait_send()
    for side in range(2):
        @pl.when(inside((0, 0, 2 * side - 1), 1))
        def _():
            slope_copy(side).wait_send()


def on_device(counts, tangent, slopes, first_kernel, second_kernel):
    ch, nx, ny, nz = tangent.shape
    lanes = ny * ch
    full = nz + 4 * PAD
    ext = nz + 2 * PAD

    def spread(array):
        return jnp.transpose(array, (1, 3, 2, 0)).reshape(nx, nz, lanes)

    def flat(array):
        return array.reshape(-1, ch)

    first_t = jnp.swapaxes(first_kernel, 1, 2)
    second_t = jnp.swapaxes(second_kernel, 1, 2)
    most = max(counts)
    result, norm = pl.pallas_call(
        functools.partial(kernel, counts, ch),
        out_shape=(
            jax.ShapeDtypeStruct((nx, nz, lanes), jnp.float32),
            jax.ShapeDtypeStruct((1, 1), jnp.float32),
        ),
        in_specs=[pl.BlockSpec(memory_space=pltpu.VMEM)] * 6,
        out_specs=(pl.BlockSpec(memory_space=pltpu.VMEM),) * 2,
        scratch_shapes=[
            pltpu.VMEM((4, nx + 2, full, lanes), jnp.bfloat16),
            pltpu.VMEM((nx, ext, lanes), jnp.bfloat16),
            pltpu.VMEM((4, 2, full, nx * ch), jnp.bfloat16),
            pltpu.VMEM((4, 2, 2, full * ch // 128, 128), jnp.bfloat16),
            pltpu.VMEM((4, 3, 2, full, nx * ch), jnp.bfloat16),
            pltpu.VMEM((4, 2, 2, full * ch // 128, 128), jnp.bfloat16),
            pltpu.VMEM((2, full, 128), jnp.bfloat16),
            pltpu.VMEM((3, nx + 2, ext, lanes), jnp.bfloat16),
            pltpu.VMEM((nx + 2, ext, lanes), jnp.bfloat16),
            pltpu.VMEM((ext, 4 * lanes), jnp.bfloat16),
            pltpu.VMEM((nx * ext, lanes), jnp.float32),
            pltpu.VMEM((27 * ch, lanes), jnp.float32),
            pltpu.VMEM((2, 12 * lanes, lanes), jnp.bfloat16),
            pltpu.VMEM((counts[0], 8, 128), jnp.float32),
            pltpu.VMEM((counts[1], 8, 128), jnp.float32),
            pltpu.VMEM((counts[2], 8, 128), jnp.float32),
            pltpu.SemaphoreType.DMA((4, len(DIRS))),
            pltpu.SemaphoreType.DMA((4, len(DIRS))),
            pltpu.SemaphoreType.DMA((2,)),
            pltpu.SemaphoreType.DMA((2,)),
            pltpu.SemaphoreType.DMA((3, most)),
            pltpu.SemaphoreType.DMA((3, most)),
        ],
        compiler_params=pltpu.CompilerParams(
            collective_id=0, has_side_effects=True, vmem_limit_bytes=48 * 1024 * 1024
        ),
        name="denoiser_step",
    )(spread(tangent), spread(slopes), flat(first_t), flat(second_t), flat(second_kernel), flat(first_kernel))
    result = result.reshape(nx, nz, ny, ch)
    return (jnp.transpose(result, (3, 0, 2, 1)), norm.reshape(1))


def solution(mesh):
    counts = tuple(mesh.shape[a] for a in AXES)
    return jax.shard_map(
        functools.partial(on_device, counts),
        mesh=mesh,
        in_specs=(P(None, "gx", "gy", "gz"), P(None, "gx", "gy", "gz"), P(), P()),
        out_specs=(P(None, "gx", "gy", "gz"), P()),
        check_vma=False,
    )
```

time: 40.3 us -> 39 us (0.968)
  Pallas kernels: 32.2 us -> 30.8 us
    pallas_call x1, Pallas kernels: 32.2 us -> 30.8 us  [on_device(): pl.pallas_call(functools.partial(kernel, counts, ch), out_shape=(jax.Shap...]
where the time goes in v2:
time: 39 us; the launch traced here: 38.7 us
  Pallas kernels  30.8 us (79%)
  local copies, waits for them, and re-layouts  5.43 us (14%)
  between operations  2.46 us (6%)
    pallas_call x1, Pallas kernels, on_device(): pl.pallas_call(functools.partial(kernel, counts, ch), out_shape=(jax.Shap...  30.8 us
    unnamed x11, local copies, waits for them, and re-layouts  3.67 us
    transpose x1, local copies, waits for them, and re-layouts, on_device(): second_t = jnp.swapaxes(second_kernel, 1, 2)  1.13 us

profile of v2, /device:TPU:0, one launch (start us, length us, event | category | flops | bytes accessed | tf_op | source)
XLA Modules:
  0.0 38.7 jit_solution(11991364815182339817)
XLA Ops:
  0.6 0.0 copy-start
  0.6 1.1 %copy.14 = bf16[27,32,32]{2,1,0:T(8,128)(2,1)S(1)} copy(bf16[27,32,32]{1,2,0:T(8,128)(2,1)} %bitcast.18) | data formatting | bytes 110592 | tf_op jit(solution)/shard_map/transpose | solution.py:329
  1.8 0.0 copy-start.2
  1.8 0.0 copy-done
  1.8 0.2 copy.13
  2.0 0.8 %copy-done.2 = bf16[32,4,8,128]{3,2,1,0:T(8,128)(2,1)S(1)} copy-done((bf16[32,4,8,128]{3,2,1,0:T(8,128)(2,1)S(1)}, bf16[32,4,8,128]{3,2,1,0:T(8,128)(2,1)}, u32[]{:S(2)}) %copy-start.2) | copy-done | bytes 262168
  2.7 0.1 copy.11
  2.8 0.0 copy-start.3
  2.8 0.1 copy.15.t_ref
  3.0 0.8 %copy-done.3 = bf16[32,4,8,128]{3,2,1,0:T(8,128)(2,1)S(1)} copy-done((bf16[32,4,8,128]{3,2,1,0:T(8,128)(2,1)S(1)}, bf16[32,4,8,128]{3,2,1,0:T(8,128)(2,1)}, u32[]{:S(2)}) %copy-start.3) | copy-done | bytes 262168
  3.8 0.1 copy.12
  3.9 0.0 copy-start.1
  3.9 0.1 copy.16.s_ref
  4.1 0.8 %copy-done.1 = bf16[27,32,32]{2,1,0:T(8,128)(2,1)S(1)} copy-done((bf16[27,32,32]{2,1,0:T(8,128)(2,1)S(1)}, bf16[27,32,32]{2,1,0:T(8,128)(2,1)}, u32[]{:S(2)}) %copy-start.1) | copy-done | bytes 55320
  4.8 30.8 %denoiser_step.1 = (f32[4,128,256]{2,1,0:T(8,128)S(1)}, f32[1,1]{1,0:T(1,128)}) custom-call(bf16[4,128,256]{2,1,0:T(8,128)(2,1)S(1)} %copy.15.t_ref, bf16[4,128,256]{2,1,0:T(8,128)(2,1)S(1)} %copy.16.s_ref, bf16[864,32]{1,0:T(8,128)(2,1)S(1)} %bitcast.21, bf16[864,32]{1,0:T(8,128)(2,1)S(1)} %bitcast.20, bf16[864,32]{1,0:T(8,128)(2,1)S(1)} %bitcast.19, ...), custom_call_target="tpu_custom_call" | custom-call | tf_op jit(solution)/shard_map/denoiser_step/pallas_call | solution.py:331
  35.6 0.2 copy.17
  35.8 1.1 %copy.18 = f32[32,4,8,128]{3,2,1,0:T(8,128)} copy(f32[32,4,8,128]{3,0,2,1:T(8,128)S(1)} %bitcast.22) | data formatting | bytes 1048576
Async XLA Ops:
  0.6 1.2 %copy-start = (bf16[27,32,32]{2,1,0:T(8,128)(2,1)S(1)}, bf16[27,32,32]{2,1,0:T(8,128)(2,1)}, u32[]{:S(2)}) copy-start(bf16[27,32,32]{2,1,0:T(8,128)(2,1)} %param.6) | copy-start | bytes 165892
  1.8 1.0 %copy-start.2 = (bf16[32,4,8,128]{3,2,1,0:T(8,128)(2,1)S(1)}, bf16[32,4,8,128]{3,2,1,0:T(8,128)(2,1)}, u32[]{:S(2)}) copy-start(bf16[32,4,8,128]{3,2,1,0:T(8,128)(2,1)} %param.4) | copy-start | bytes 786436
  2.8 1.0 %copy-start.3 = (bf16[32,4,8,128]{3,2,1,0:T(8,128)(2,1)S(1)}, bf16[32,4,8,128]{3,2,1,0:T(8,128)(2,1)}, u32[]{:S(2)}) copy-start(bf16[32,4,8,128]{3,2,1,0:T(8,128)(2,1)} %param.5) | copy-start | bytes 786436
  3.9 0.9 %copy-start.1 = (bf16[27,32,32]{2,1,0:T(8,128)(2,1)S(1)}, bf16[27,32,32]{2,1,0:T(8,128)(2,1)}, u32[]{:S(2)}) copy-start(bf16[27,32,32]{2,1,0:T(8,128)(2,1)} %param.7) | copy-start | bytes 165892

commit v3 on v2

--- a/solution.py
+++ b/solution.py
@@ -18,13 +18,13 @@
 
 
 def kernel(
-    counts, ch, t_ref, s_ref, k1t_ref, k2t_ref, k2_ref, k1_ref, out_ref, norm_ref,
+    counts, t_hbm, s_hbm, k1_hbm, k2_hbm, out_ref, norm_ref, t_in, s_in, k1_in, k2_in,
     field, slopes, edge, edge_x, rows, rows_x, line,
     shifted, shifted_y, shifted_x, acc, taps, weights, sums_x, sums_y, sums_z,
-    send_sem, recv_sem, slope_send, slope_recv, sum_send, sum_recv,
+    load_sem, send_sem, recv_sem, slope_send, slope_recv, sum_send, sum_recv,
 ):
-    nx, nz, lanes = t_ref.shape
-    ny = lanes // ch
+    ch, nx, ny, nz = t_in.shape
+    lanes = ny * ch
     ext = nz + 2 * PAD
     own = 2 * PAD
     parts = 128 // ch
@@ -46,6 +46,15 @@
             there = list(me)
             there[axis] = lax.rem(me[axis] + k, n)
             yield k, tuple(there)
+
+    loads = [
+        pltpu.make_async_copy(src, dst, load_sem.at[j])
+        for j, (src, dst) in enumerate(
+            ((k1_hbm, k1_in), (t_hbm, t_in), (s_hbm, s_in), (k2_hbm, k2_in))
+        )
+    ]
+    for load in loads:
+        load.start()
 
     for buf in (field, slopes, rows, rows_x, line, shifted, shifted_y, shifted_x, weights):
         buf[...] = jnp.zeros_like(buf)
@@ -134,14 +143,22 @@
             result = result + buf[j]
         return result
 
-    lane_block = lax.broadcasted_iota(jnp.int32, (ch, lanes), 1) // ch
-    lane_inner = lax.rem(lax.broadcasted_iota(jnp.int32, (ch, lanes), 1), ch)
-    tiler = (lax.broadcasted_iota(jnp.int32, (ch, lanes), 0) == lane_inner)
+    half = 128
+    lane_block = lax.broadcasted_iota(jnp.int32, (ch, half), 1) // ch
+    lane_inner = lax.rem(lax.broadcasted_iota(jnp.int32, (ch, half), 1), ch)
+    tiler = (lax.broadcasted_iota(jnp.int32, (ch, half), 0) == lane_inner)
     tiler = tiler.astype(jnp.float32).astype(jnp.bfloat16)
 
     def build(r):
-        k_ref, flip = ((k1t_ref, 0), (k2t_ref, 0), (k2_ref, 1), (k1_ref, 1))[r]
-        taps[...] = jnp.dot(k_ref[...], tiler, preferred_element_type=jnp.float32)
+        k_in, flip = ((k1_in, 0), (k2_in, 0), (k2_in, 1), (k1_in, 1))[r]
+        if flip:
+            flat = k_in[...].reshape(27 * ch, ch)
+            taps[...] = jnp.dot(flat, tiler, preferred_element_type=jnp.float32)
+        else:
+            for t in range(27):
+                taps[t * ch : (t + 1) * ch, :] = lax.dot_general(
+                    k_in[t], tiler, (((0,), (0,)), ((), ())), preferred_element_type=jnp.float32
+                )
 
         def group(g, carry):
             mats = []
@@ -149,23 +166,33 @@
                 tap = 9 * (g // 3) + 3 * b + g % 3
                 tap = 26 - tap if flip else tap
                 mats.append(taps[pl.ds(pl.multiple_of(tap * ch, ch), ch), :])
-            strips = []
-            for y in list(range(ny)) + [-1, ny]:
-                strip = jnp.zeros((ch, lanes), jnp.float32)
+
+            def strip(y, h):
+                tile = jnp.zeros((ch, half), jnp.float32)
                 for b in range(3):
-                    if 0 <= y - (b - 1) < ny:
-                        strip = jnp.where(lane_block == y - (b - 1), mats[b], strip)
-                strips.append(strip)
+                    to = y - (b - 1)
+                    if 0 <= to < ny and to // parts == h:
+                        tile = jnp.where(lane_block == to % parts, mats[b], tile)
+                return tile.astype(jnp.bfloat16)
+
             base = per_a * (g // 3)
-            at = pl.multiple_of(base + lanes * (g % 3), ch)
-            main = jnp.concatenate(strips[:ny], axis=0)
-            weights[r % 2, pl.ds(at, lanes), :] = main.astype(jnp.bfloat16)
+            for h in range(lanes // half):
+                y_from, y_to = max(0, h * parts - 1), min(ny, (h + 1) * parts + 1)
+                at = pl.multiple_of(base + lanes * (g % 3) + y_from * ch, ch)
+                weights[r % 2, pl.ds(at, (y_to - y_from) * ch), h * half : (h + 1) * half] = (
+                    jnp.concatenate([strip(y, h) for y in range(y_from, y_to)], axis=0)
+                )
             at = pl.multiple_of(base + 3 * lanes + 2 * ch * (g % 3), ch)
-            outer = jnp.concatenate(strips[ny:], axis=0)
-            weights[r % 2, pl.ds(at, 2 * ch), :] = outer.astype(jnp.bfloat16)
+            weights[r % 2, pl.ds(at, ch), 0:half] = strip(-1, 0)
+            at = pl.multiple_of(at + ch, ch)
+            weights[r % 2, pl.ds(at, ch), lanes - half : lanes] = strip(ny, lanes // half - 1)
             return carry
 
         lax.fori_loop(0, 9, group, 0)
+
+    def spread(ref, x):
+        block = jnp.transpose(ref[:, x].astype(jnp.float32), (1, 0, 2))
+        return jnp.transpose(block.reshape(lanes, nz), (1, 0)).astype(jnp.bfloat16)
 
     def conv(r):
         z, size = (own, nz) if r == 0 else (PAD, ext)
@@ -185,7 +212,6 @@
                         r, 1 + x, z : z + piece, low : low + ch
                     ]
         if r == 0:
-            build(0)
             pl.semaphore_wait(barrier, total)
         for i, d in dirs_of(r):
             @pl.when(inside(d, 1))
@@ -200,6 +226,9 @@
                         copy_of(r, i).wait_recv()
 
         if r == 0:
+            loads[2].wait()
+            for x in range(nx):
+                slopes[x, PAD : PAD + nz, :] = spread(s_in, x)
             for side in range(2):
                 @pl.when(inside((0, 0, 2 * side - 1), 1))
                 def _():
@@ -225,6 +254,8 @@
             jnp.concatenate(pieces, axis=1), weight_rows(0, 3 * lanes),
             preferred_element_type=jnp.float32,
         )
+        if r == 0:
+            loads[3].wait()
         if r < 3:
             build(r + 1)
         arrive(lambda d: d[0] == 0 and d[1] != 0)
@@ -275,8 +306,11 @@
                 )
         return acc[0 : nx * size, :].reshape(nx, size, lanes)
 
-    slopes[:, PAD : PAD + nz, :] = s_ref[...]
-    field[0, 1 : nx + 1, own : own + nz, :] = t_ref[...]
+    loads[0].wait()
+    build(0)
+    loads[1].wait()
+    for x in range(nx):
+        field[0, 1 + x, own : own + nz, :] = spread(t_in, x)
     inner = conv(0)
     for side in range(2):
         @pl.when(inside((0, 0, 2 * side - 1), -1))
@@ -319,24 +353,20 @@
     full = nz + 4 * PAD
     ext = nz + 2 * PAD
 
-    def spread(array):
-        return jnp.transpose(array, (1, 3, 2, 0)).reshape(nx, nz, lanes)
-
-    def flat(array):
-        return array.reshape(-1, ch)
-
-    first_t = jnp.swapaxes(first_kernel, 1, 2)
-    second_t = jnp.swapaxes(second_kernel, 1, 2)
     most = max(counts)
     result, norm = pl.pallas_call(
-        functools.partial(kernel, counts, ch),
+        functools.partial(kernel, counts),
         out_shape=(
             jax.ShapeDtypeStruct((nx, nz, lanes), jnp.float32),
             jax.ShapeDtypeStruct((1, 1), jnp.float32),
         ),
-        in_specs=[pl.BlockSpec(memory_space=pltpu.VMEM)] * 6,
+        in_specs=[pl.BlockSpec(memory_space=pl.ANY)] * 4,
         out_specs=(pl.BlockSpec(memory_space=pltpu.VMEM),) * 2,
         scratch_shapes=[
+            pltpu.VMEM(tangent.shape, jnp.bfloat16),
+            pltpu.VMEM(slopes.shape, jnp.bfloat16),
+            pltpu.VMEM(first_kernel.shape, jnp.bfloat16),
+            pltpu.VMEM(second_kernel.shape, jnp.bfloat16),
             pltpu.VMEM((4, nx + 2, full, lanes), jnp.bfloat16),
             pltpu.VMEM((nx, ext, lanes), jnp.bfloat16),
             pltpu.VMEM((4, 2, full, nx * ch), jnp.bfloat16),
@@ -348,11 +378,12 @@
             pltpu.VMEM((nx + 2, ext, lanes), jnp.bfloat16),
             pltpu.VMEM((ext, 4 * lanes), jnp.bfloat16),
             pltpu.VMEM((nx * ext, lanes), jnp.float32),
-            pltpu.VMEM((27 * ch, lanes), jnp.float32),
+            pltpu.VMEM((27 * ch, 128), jnp.float32),
             pltpu.VMEM((2, 12 * lanes, lanes), jnp.bfloat16),
             pltpu.VMEM((counts[0], 8, 128), jnp.float32),
             pltpu.VMEM((counts[1], 8, 128), jnp.float32),
             pltpu.VMEM((counts[2], 8, 128), jnp.float32),
+            pltpu.SemaphoreType.DMA((4,)),
             pltpu.SemaphoreType.DMA((4, len(DIRS))),
             pltpu.SemaphoreType.DMA((4, len(DIRS))),
             pltpu.SemaphoreType.DMA((2,)),
@@ -364,7 +395,7 @@
             collective_id=0, has_side_effects=True, vmem_limit_bytes=48 * 1024 * 1024
         ),
         name="denoiser_step",
-    )(spread(tangent), spread(slopes), flat(first_t), flat(second_t), flat(second_kernel), flat(first_kernel))
+    )(tangent, slopes, first_kernel, second_kernel)
     result = result.reshape(nx, nz, ny, ch)
     return (jnp.transpose(result, (3, 0, 2, 1)), norm.reshape(1))
 

time: 39 us -> 39.2 us (level)
  Pallas kernels: 30.8 us -> 31.4 us
    transpose x2 -> x0, local copies, waits for them, and re-layouts: 1.28 us -> none  [the longest x1 1.13 us: on_device(): second_t = jnp.swapaxes(second_kernel, 1, 2)]
    unnamed x11 -> x9, local copies, waits for them, and re-layouts: 3.67 us -> 4.87 us
    pallas_call x1, Pallas kernels: 30.8 us -> 31.4 us  [on_device(): pl.pallas_call(functools.partial(kernel, counts), out_shape=(jax.ShapeDty...]
where the time goes in v3:
time: 39.2 us; the launch traced here: 38.9 us
  Pallas kernels  31.4 us (80%)
  local copies, waits for them, and re-layouts  5.06 us (13%)
  between operations  2.41 us (6%)
    pallas_call x1, Pallas kernels, on_device(): pl.pallas_call(functools.partial(kernel, counts), out_shape=(jax.ShapeDty...  31.4 us
    unnamed x9, local copies, waits for them, and re-layouts  4.87 us

profile of v3, /device:TPU:0, one launch (start us, length us, event | category | flops | bytes accessed | tf_op | source)
XLA Modules:
  0.0 38.9 jit_solution(7089495286501486761)
XLA Ops:
  0.6 0.0 copy-start
  0.6 0.9 %copy-done = bf16[32,4,8,128]{3,2,1,0:T(8,128)(2,1)S(1)} copy-done((bf16[32,4,8,128]{3,2,1,0:T(8,128)(2,1)S(1)}, bf16[32,4,8,128]{3,2,1,0:T(8,128)(2,1)}, u32[]{:S(2)}) %copy-start) | copy-done | bytes 262168
  1.6 0.0 copy-start.1
  1.6 0.9 %copy-done.1 = bf16[32,4,8,128]{3,2,1,0:T(8,128)(2,1)S(1)} copy-done((bf16[32,4,8,128]{3,2,1,0:T(8,128)(2,1)S(1)}, bf16[32,4,8,128]{3,2,1,0:T(8,128)(2,1)}, u32[]{:S(2)}) %copy-start.1) | copy-done | bytes 262168
  2.5 0.0 copy-start.2
  2.5 0.9 %copy-done.2 = bf16[27,32,32]{2,1,0:T(8,128)(2,1)S(1)} copy-done((bf16[27,32,32]{2,1,0:T(8,128)(2,1)S(1)}, bf16[27,32,32]{2,1,0:T(8,128)(2,1)}, u32[]{:S(2)}) %copy-start.2) | copy-done | bytes 55320
  3.5 0.0 copy-start.3
  3.5 0.9 %copy-done.3 = bf16[27,32,32]{2,1,0:T(8,128)(2,1)S(1)} copy-done((bf16[27,32,32]{2,1,0:T(8,128)(2,1)S(1)}, bf16[27,32,32]{2,1,0:T(8,128)(2,1)}, u32[]{:S(2)}) %copy-start.3) | copy-done | bytes 55320
  4.4 31.4 %denoiser_step.1 = (f32[4,128,256]{2,1,0:T(8,128)S(1)}, f32[1,1]{1,0:T(1,128)}) custom-call(bf16[32,4,8,128]{3,2,1,0:T(8,128)(2,1)S(1)} %copy-done, bf16[32,4,8,128]{3,2,1,0:T(8,128)(2,1)S(1)} %copy-done.1, bf16[27,32,32]{2,1,0:T(8,128)(2,1)S(1)} %copy-done.2, bf16[27,32,32]{2,1,0:T(8,128)(2,1)S(1)} %copy-done.3), custom_call_target="tpu_custom_call" | custom-call | tf_op jit(solution)/shard_map/denoiser_step/pallas_call | solution.py:357
  35.8 0.2 copy.7
  36.0 1.1 %copy.8 = f32[32,4,8,128]{3,2,1,0:T(8,128)} copy(f32[32,4,8,128]{3,0,2,1:T(8,128)S(1)} %bitcast.4) | data formatting | bytes 1048576
Async XLA Ops:
  0.6 1.0 %copy-start = (bf16[32,4,8,128]{3,2,1,0:T(8,128)(2,1)S(1)}, bf16[32,4,8,128]{3,2,1,0:T(8,128)(2,1)}, u32[]{:S(2)}) copy-start(bf16[32,4,8,128]{3,2,1,0:T(8,128)(2,1)} %t_hbm.1) | copy-start | bytes 786436
  1.6 0.9 %copy-start.1 = (bf16[32,4,8,128]{3,2,1,0:T(8,128)(2,1)S(1)}, bf16[32,4,8,128]{3,2,1,0:T(8,128)(2,1)}, u32[]{:S(2)}) copy-start(bf16[32,4,8,128]{3,2,1,0:T(8,128)(2,1)} %s_hbm.1) | copy-start | bytes 786436
  2.5 0.9 %copy-start.2 = (bf16[27,32,32]{2,1,0:T(8,128)(2,1)S(1)}, bf16[27,32,32]{2,1,0:T(8,128)(2,1)}, u32[]{:S(2)}) copy-start(bf16[27,32,32]{2,1,0:T(8,128)(2,1)} %k1_hbm.1) | copy-start | bytes 165892
  3.5 0.9 %copy-start.3 = (bf16[27,32,32]{2,1,0:T(8,128)(2,1)S(1)}, bf16[27,32,32]{2,1,0:T(8,128)(2,1)}, u32[]{:S(2)}) copy-start(bf16[27,32,32]{2,1,0:T(8,128)(2,1)} %k2_hbm.1) | copy-start | bytes 165892

commit v4 on v3

--- a/solution.py
+++ b/solution.py
@@ -194,7 +194,29 @@
         block = jnp.transpose(ref[:, x].astype(jnp.float32), (1, 0, 2))
         return jnp.transpose(block.reshape(lanes, nz), (1, 0)).astype(jnp.bfloat16)
 
-    def conv(r):
+    def span(r):
+        return (own, nz // parts) if r == 0 else (0, (nz + 4 * PAD) // parts)
+
+    def send(r, keep):
+        for i, d in dirs_of(r):
+            if keep(d):
+                @pl.when(inside(d, 1))
+                def _():
+                    copy_of(r, i).start()
+
+    def send_face(r, side):
+        start, piece = span(r)
+        x = nx - 1 if side else 0
+        for s in range(2):
+            low = s * (ny - 1) * ch
+            for q in range(parts):
+                z = start + q * piece
+                edge_x[r, side, s, 0:piece, q * ch : (q + 1) * ch] = field[
+                    r, 1 + x, z : z + piece, low : low + ch
+                ]
+        send(r, lambda d: d[0] == 2 * side - 1 and d[2] == 0)
+
+    def send_rest(r):
         z, size = (own, nz) if r == 0 else (PAD, ext)
         for s in range(2):
             low = s * (ny - 1) * ch
@@ -202,21 +224,23 @@
                 edge[r, s, z : z + size, x * ch : (x + 1) * ch] = field[
                     r, 1 + x, z : z + size, low : low + ch
                 ]
-        start, piece = (own, nz // parts) if r == 0 else (0, (nz + 4 * PAD) // parts)
-        for s in range(2):
-            low = s * (ny - 1) * ch
-            for side, x in enumerate((0, nx - 1)):
-                for q in range(parts):
-                    z = start + q * piece
-                    edge_x[r, side, s, 0:piece, q * ch : (q + 1) * ch] = field[
-                        r, 1 + x, z : z + piece, low : low + ch
-                    ]
-        if r == 0:
-            pl.semaphore_wait(barrier, total)
-        for i, d in dirs_of(r):
-            @pl.when(inside(d, 1))
-            def _():
-                copy_of(r, i).start()
+        send(r, lambda d: d[0] == 0 or d[2] != 0)
+
+    def emit(r, x):
+        if r == 3:
+            return
+        value = acc[x * ext : (x + 1) * ext, :]
+        if r == 1:
+            row = lax.broadcasted_iota(jnp.int32, (ext, lanes), 0)
+            first = jnp.where(me[2] == 0, PAD, 0)
+            last = jnp.where(me[2] == counts[2] - 1, PAD + nz, ext)
+            value = jnp.where(jnp.logical_and(row >= first, row < last), value, 0.0)
+        else:
+            value = slopes[x].astype(jnp.float32) * value
+        field[r + 1, 1 + x, PAD : PAD + ext, :] = value.astype(jnp.bfloat16)
+
+    def conv(r):
+        start, piece = span(r)
 
         def arrive(keep):
             for i, d in dirs_of(r):
@@ -274,10 +298,23 @@
             jnp.concatenate(pieces, axis=1), weight_rows(3 * lanes, lanes),
             preferred_element_type=jnp.float32,
         )
+        if r == 0:
+            for side in range(2):
+                @pl.when(inside((0, 0, 2 * side - 1), -1))
+                def _():
+                    slope_copy(side).wait_recv()
         if r == 2:
             start_sum(1, sums_y, finish_sum(0, sums_x))
+        faces = ((1, 0, 0, 0), (0, nx + 1, nx - 1, 2))
+        for x in range(1, nx - 1):
+            emit(r, x)
+        for side, plane, out, a in faces:
+            @pl.when(jnp.logical_not(inside((2 * side - 1, 0, 0), -1)))
+            def _():
+                emit(r, out)
+
         arrive(lambda d: d[0] != 0)
-        for side, plane, out, a in ((1, 0, 0, 0), (0, nx + 1, nx - 1, 2)):
+        for side, plane, out, a in faces:
             @pl.when(inside((2 * side - 1, 0, 0), -1))
             def _():
                 x = nx - 1 if side else 0
@@ -304,37 +341,35 @@
                     shifted_x[lo : lo + size, :], weights[r % 2, a * per_a : (a + 1) * per_a, :],
                     preferred_element_type=jnp.float32,
                 )
-        return acc[0 : nx * size, :].reshape(nx, size, lanes)
+                emit(r, out)
+                if r < 3:
+                    send_face(r + 1, 1 - side)
+
+        if r < 3:
+            send_rest(r + 1)
 
     loads[0].wait()
     build(0)
     loads[1].wait()
     for x in range(nx):
         field[0, 1 + x, own : own + nz, :] = spread(t_in, x)
-    inner = conv(0)
+    pl.semaphore_wait(barrier, total)
     for side in range(2):
-        @pl.when(inside((0, 0, 2 * side - 1), -1))
-        def _():
-            slope_copy(side).wait_recv()
-    hidden = slopes[...].astype(jnp.float32) * inner
-    field[1, 1 : nx + 1, PAD : PAD + ext, :] = hidden.astype(jnp.bfloat16)
-    image = conv(1)
-    row = lax.broadcasted_iota(jnp.int32, (1, ext, lanes), 1)
-    first = jnp.where(me[2] == 0, PAD, 0)
-    last = jnp.where(me[2] == counts[2] - 1, PAD + nz, ext)
-    low_image = jnp.where(jnp.logical_and(row >= first, row < last), image, 0.0)
-    field[2, 1 : nx + 1, PAD : PAD + ext, :] = low_image.astype(jnp.bfloat16)
-    part = image[:, PAD : PAD + nz, :].reshape(nx * nz // 8, 8, lanes)
-    squares = jnp.sum(part * part, axis=0)
+        send_face(0, side)
+    send_rest(0)
+    conv(0)
+    conv(1)
+    squares = jnp.zeros((8, lanes), jnp.float32)
+    for x in range(nx):
+        part = acc[x * ext + PAD : x * ext + PAD + nz, :].reshape(nz // 8, 8, lanes)
+        squares = squares + jnp.sum(part * part, axis=0)
     start_sum(0, sums_x, sum(squares[:, j : j + 128] for j in range(0, lanes, 128)))
-    back = conv(2)
+    conv(2)
     start_sum(2, sums_z, finish_sum(1, sums_y))
-    pulled = slopes[...].astype(jnp.float32) * back
-    field[3, 1 : nx + 1, PAD : PAD + ext, :] = pulled.astype(jnp.bfloat16)
-    result = conv(3)
+    conv(3)
     norm = jnp.sqrt(jnp.sum(finish_sum(2, sums_z), keepdims=True) + 1e-06)
     norm_ref[...] = norm
-    out_ref[...] = result / norm.reshape(1, 1, 1)
+    out_ref[...] = (acc[0 : nx * nz, :] / norm).reshape(nx, nz, lanes)
 
     for r in range(4):
         for i, d in dirs_of(r):
@@ -392,7 +427,7 @@
             pltpu.SemaphoreType.DMA((3, most)),
         ],
         compiler_params=pltpu.CompilerParams(
-            collective_id=0, has_side_effects=True, vmem_limit_bytes=48 * 1024 * 1024
+            collective_id=0, has_side_effects=True, vmem_limit_bytes=56 * 1024 * 1024
         ),
         name="denoiser_step",
     )(tangent, slopes, first_kernel, second_kernel)

time: 39.2 us -> 35.7 us (0.911)
  local copies, waits for them, and re-layouts: 5.06 us -> 2.34 us
  Pallas kernels: 31.4 us -> 30.8 us
    unnamed x9 -> x1, local copies, waits for them, and re-layouts: 4.87 us -> 1.11 us
    pallas_call x1, local copies, waits for them, and re-layouts: 0.19 us -> 1.23 us  [on_device(): pl.pallas_call(functools.partial(kernel, counts), out_shape=(jax.ShapeDty...]
    pallas_call x1, Pallas kernels: 31.4 us -> 30.8 us  [on_device(): pl.pallas_call(functools.partial(kernel, counts), out_shape=(jax.ShapeDty...]
where the time goes in v4:
time: 35.7 us; the launch traced here: 35.5 us
  Pallas kernels  30.8 us (86%)
  local copies, waits for them, and re-layouts  2.34 us (7%)
  between operations  2.34 us (7%)
    pallas_call x1, Pallas kernels, on_device(): pl.pallas_call(functools.partial(kernel, counts), out_shape=(jax.ShapeDty...  30.8 us
    pallas_call x1, local copies, waits for them, and re-layouts, on_device(): pl.pallas_call(functools.partial(kernel, counts), out_shape=(jax.ShapeDty...  1.23 us
    unnamed x1, local copies, waits for them, and re-layouts  1.11 us

profile of v4, /device:TPU:0, one launch (start us, length us, event | category | flops | bytes accessed | tf_op | source)
XLA Modules:
  0.0 35.5 jit_solution(7160789674502694411)
XLA Ops:
  0.6 30.8 %denoiser_step.1 = (f32[4,128,256]{2,1,0:T(8,128)}, f32[1,1]{1,0:T(1,128)}) custom-call(bf16[32,4,8,128]{3,2,1,0:T(8,128)(2,1)} %t_hbm.1, bf16[32,4,8,128]{3,2,1,0:T(8,128)(2,1)} %s_hbm.1, bf16[27,32,32]{2,1,0:T(8,128)(2,1)} %k1_hbm.1, bf16[27,32,32]{2,1,0:T(8,128)(2,1)} %k2_hbm.1), custom_call_target="tpu_custom_call" | custom-call | tf_op jit(solution)/shard_map/denoiser_step/pallas_call | solution.py:392
  31.4 1.2 %copy.7 = f32[4,128,256]{1,2,0:T(8,128)S(1)} copy(f32[4,128,256]{2,1,0:T(8,128)} %get-tuple-element.4) | data formatting | bytes 1048576 | tf_op jit(solution)/shard_map/denoiser_step/pallas_call | solution.py:392
  32.7 1.1 %copy.8 = f32[32,4,8,128]{3,2,1,0:T(8,128)} copy(f32[32,4,8,128]{3,0,2,1:T(8,128)S(1)} %bitcast.4) | data formatting | bytes 1048576

commit v5 on v4

--- a/solution.py
+++ b/solution.py
@@ -50,14 +50,22 @@
     loads = [
         pltpu.make_async_copy(src, dst, load_sem.at[j])
         for j, (src, dst) in enumerate(
-            ((k1_hbm, k1_in), (t_hbm, t_in), (s_hbm, s_in), (k2_hbm, k2_in))
+            ((t_hbm, t_in), (s_hbm, s_in), (k1_hbm, k1_in), (k2_hbm, k2_in))
         )
     ]
     for load in loads:
         load.start()
 
-    for buf in (field, slopes, rows, rows_x, line, shifted, shifted_y, shifted_x, weights):
-        buf[...] = jnp.zeros_like(buf)
+    def clear(*refs):
+        for ref in refs:
+            ref[...] = jnp.zeros(ref.shape, ref.dtype)
+
+    clear(rows, rows_x)
+    clear(field.at[:, 0], field.at[:, nx + 1])
+    for z in (0, own + nz):
+        clear(field.at[:, pl.ds(1, nx), pl.ds(z, own), :])
+    for z in (0, PAD + nz):
+        clear(slopes.at[:, pl.ds(z, PAD), :])
 
     barrier = pltpu.get_barrier_semaphore()
     total = jnp.int32(0)
@@ -226,8 +234,10 @@
                 ]
         send(r, lambda d: d[0] == 0 or d[2] != 0)
 
-    def emit(r, x):
+    def emit(r, x, norm):
         if r == 3:
+            block = jnp.transpose(acc[x * nz : (x + 1) * nz, :] / norm, (1, 0))
+            out_ref[:, x] = jnp.transpose(block.reshape(ny, ch, nz), (1, 0, 2))
             return
         value = acc[x * ext : (x + 1) * ext, :]
         if r == 1:
@@ -250,7 +260,7 @@
                         copy_of(r, i).wait_recv()
 
         if r == 0:
-            loads[2].wait()
+            loads[1].wait()
             for x in range(nx):
                 slopes[x, PAD : PAD + nz, :] = spread(s_in, x)
             for side in range(2):
@@ -305,13 +315,17 @@
                     slope_copy(side).wait_recv()
         if r == 2:
             start_sum(1, sums_y, finish_sum(0, sums_x))
+        norm = None
+        if r == 3:
+            norm = jnp.sqrt(jnp.sum(finish_sum(2, sums_z), keepdims=True) + 1e-06)
+            norm_ref[...] = norm
         faces = ((1, 0, 0, 0), (0, nx + 1, nx - 1, 2))
         for x in range(1, nx - 1):
-            emit(r, x)
+            emit(r, x, norm)
         for side, plane, out, a in faces:
             @pl.when(jnp.logical_not(inside((2 * side - 1, 0, 0), -1)))
             def _():
-                emit(r, out)
+                emit(r, out, norm)
 
         arrive(lambda d: d[0] != 0)
         for side, plane, out, a in faces:
@@ -341,7 +355,7 @@
                     shifted_x[lo : lo + size, :], weights[r % 2, a * per_a : (a + 1) * per_a, :],
                     preferred_element_type=jnp.float32,
                 )
-                emit(r, out)
+                emit(r, out, norm)
                 if r < 3:
                     send_face(r + 1, 1 - side)
 
@@ -349,14 +363,18 @@
             send_rest(r + 1)
 
     loads[0].wait()
-    build(0)
-    loads[1].wait()
-    for x in range(nx):
+    for x in (0, nx - 1):
         field[0, 1 + x, own : own + nz, :] = spread(t_in, x)
     pl.semaphore_wait(barrier, total)
     for side in range(2):
         send_face(0, side)
+    for x in range(1, nx - 1):
+        field[0, 1 + x, own : own + nz, :] = spread(t_in, x)
     send_rest(0)
+    clear(line, shifted_x, weights, shifted_y)
+    clear(shifted.at[:, 0], shifted.at[:, nx + 1])
+    loads[2].wait()
+    build(0)
     conv(0)
     conv(1)
     squares = jnp.zeros((8, lanes), jnp.float32)
@@ -367,9 +385,6 @@
     conv(2)
     start_sum(2, sums_z, finish_sum(1, sums_y))
     conv(3)
-    norm = jnp.sqrt(jnp.sum(finish_sum(2, sums_z), keepdims=True) + 1e-06)
-    norm_ref[...] = norm
-    out_ref[...] = (acc[0 : nx * nz, :] / norm).reshape(nx, nz, lanes)
 
     for r in range(4):
         for i, d in dirs_of(r):
@@ -392,7 +407,7 @@
     result, norm = pl.pallas_call(
         functools.partial(kernel, counts),
         out_shape=(
-            jax.ShapeDtypeStruct((nx, nz, lanes), jnp.float32),
+            jax.ShapeDtypeStruct(tangent.shape, jnp.float32),
             jax.ShapeDtypeStruct((1, 1), jnp.float32),
         ),
         in_specs=[pl.BlockSpec(memory_space=pl.ANY)] * 4,
@@ -431,8 +446,7 @@
         ),
         name="denoiser_step",
     )(tangent, slopes, first_kernel, second_kernel)
-    result = result.reshape(nx, nz, ny, ch)
-    return (jnp.transpose(result, (3, 0, 2, 1)), norm.reshape(1))
+    return (result, norm.reshape(1))
 
 
 def solution(mesh):

time: 35.7 us -> 35.6 us (level)
  local copies, waits for them, and re-layouts: 2.34 us -> 1.87 us
  Pallas kernels: 30.8 us -> 31.2 us
    pallas_call x1 -> x0, local copies, waits for them, and re-layouts: 1.23 us -> none  [on_device(): pl.pallas_call(functools.partial(kernel, counts), out_shape=(jax.ShapeDty...]
    unnamed x1, local copies, waits for them, and re-layouts: 1.11 us -> 1.87 us
    pallas_call x1, Pallas kernels: 30.8 us -> 31.2 us  [on_device(): pl.pallas_call(functools.partial(kernel, counts), out_shape=(jax.ShapeDty...]
where the time goes in v5:
time: 35.6 us; the launch traced here: 35.4 us
  Pallas kernels  31.2 us (88%)
  between operations  2.34 us (7%)
  local copies, waits for them, and re-layouts  1.87 us (5%)
    pallas_call x1, Pallas kernels, on_device(): pl.pallas_call(functools.partial(kernel, counts), out_shape=(jax.ShapeDty...  31.2 us
    unnamed x1, local copies, waits for them, and re-layouts  1.87 us

profile of v5, /device:TPU:0, one launch (start us, length us, event | category | flops | bytes accessed | tf_op | source)
XLA Modules:
  0.0 35.4 jit_solution(15875452954562307981)
XLA Ops:
  0.6 31.2 %denoiser_step.1 = (f32[32,4,8,128]{3,2,1,0:T(8,128)}, f32[1,1]{1,0:T(1,128)}) custom-call(bf16[32,4,8,128]{3,2,1,0:T(8,128)(2,1)} %t_hbm.1, bf16[32,4,8,128]{3,2,1,0:T(8,128)(2,1)} %s_hbm.1, bf16[27,32,32]{2,1,0:T(8,128)(2,1)} %k1_hbm.1, bf16[27,32,32]{2,1,0:T(8,128)(2,1)} %k2_hbm.1), custom_call_target="tpu_custom_call" | custom-call | tf_op jit(solution)/shard_map/denoiser_step/pallas_call | solution.py:407
  31.8 1.9 %copy.8 = f32[32,4,8,128]{3,2,1,0:T(8,128)} copy(f32[32,4,8,128]{3,2,1,0:T(8,128)} %get-tuple-element.8) | data formatting | bytes 1048576

commit v6 on v5

--- a/solution.py
+++ b/solution.py
@@ -234,20 +234,24 @@
                 ]
         send(r, lambda d: d[0] == 0 or d[2] != 0)
 
+    def rows_of(r):
+        return (PAD, nz) if r == 3 else (PAD // 2, nz + PAD)
+
     def emit(r, x, norm):
         if r == 3:
             block = jnp.transpose(acc[x * nz : (x + 1) * nz, :] / norm, (1, 0))
             out_ref[:, x] = jnp.transpose(block.reshape(ny, ch, nz), (1, 0, 2))
             return
-        value = acc[x * ext : (x + 1) * ext, :]
+        lo, size = rows_of(r)
+        value = acc[x * size : (x + 1) * size, :]
         if r == 1:
-            row = lax.broadcasted_iota(jnp.int32, (ext, lanes), 0)
+            row = lax.broadcasted_iota(jnp.int32, (size, lanes), 0) + lo
             first = jnp.where(me[2] == 0, PAD, 0)
             last = jnp.where(me[2] == counts[2] - 1, PAD + nz, ext)
             value = jnp.where(jnp.logical_and(row >= first, row < last), value, 0.0)
         else:
-            value = slopes[x].astype(jnp.float32) * value
-        field[r + 1, 1 + x, PAD : PAD + ext, :] = value.astype(jnp.bfloat16)
+            value = slopes[x, lo : lo + size, :].astype(jnp.float32) * value
+        field[r + 1, 1 + x, PAD + lo : PAD + lo + size, :] = value.astype(jnp.bfloat16)
 
     def conv(r):
         start, piece = span(r)
@@ -269,25 +273,20 @@
                     slope_copy(side).start()
 
         arrive(lambda d: d[0] == 0 and d[1] == 0)
-        lo, size = (PAD, nz) if r == 3 else (0, ext)
+        lo, size = rows_of(r)
         for c in range(3):
             z = PAD - 1 + c + lo
-            shifted[c, 1 : nx + 1, lo : lo + size, :] = field[r, 1 : nx + 1, z : z + size, :]
-
-        def weight_rows(first, count):
-            return jnp.concatenate(
-                [weights[r % 2, a * per_a + first : a * per_a + first + count, :] for a in range(3)],
-                axis=0,
-            )
-
-        pieces = [
-            shifted[c, a : a + nx, lo : lo + size, :].reshape(nx * size, lanes)
-            for a in range(3) for c in range(3)
-        ]
-        acc[0 : nx * size, :] = jnp.dot(
-            jnp.concatenate(pieces, axis=1), weight_rows(0, 3 * lanes),
-            preferred_element_type=jnp.float32,
-        )
+            shifted[1 : nx + 1, 0:size, c * lanes : (c + 1) * lanes] = field[
+                r, 1 : nx + 1, z : z + size, :
+            ]
+
+        def planes_dot(buf, a, first):
+            lhs = buf[a : a + nx, 0:size, :].reshape(nx * size, buf.shape[2])
+            base = a * per_a + first
+            rhs = weights[r % 2, base : base + buf.shape[2], :]
+            return jnp.dot(lhs, rhs, preferred_element_type=jnp.float32)
+
+        acc[0 : nx * size, :] = sum(planes_dot(shifted, a, 0) for a in range(3))
         if r == 0:
             loads[3].wait()
         if r < 3:
@@ -298,16 +297,10 @@
             for s in range(2):
                 low = (2 * c + s) * ch
                 for x in range(nx):
-                    shifted_y[1 + x, lo : lo + size, low : low + ch] = rows[
+                    shifted_y[1 + x, 0:size, low : low + ch] = rows[
                         r, 1, s, z : z + size, x * ch : (x + 1) * ch
                     ]
-        pieces = [
-            shifted_y[a : a + nx, lo : lo + size, :].reshape(nx * size, lanes) for a in range(3)
-        ]
-        acc[0 : nx * size, :] += jnp.dot(
-            jnp.concatenate(pieces, axis=1), weight_rows(3 * lanes, lanes),
-            preferred_element_type=jnp.float32,
-        )
+        acc[0 : nx * size, :] += sum(planes_dot(shifted_y, a, 3 * lanes) for a in range(3))
         if r == 0:
             for side in range(2):
                 @pl.when(inside((0, 0, 2 * side - 1), -1))
@@ -345,14 +338,14 @@
                         ]
                 for c in range(3):
                     z = PAD - 1 + c + lo
-                    shifted_x[lo : lo + size, c * lanes : (c + 1) * lanes] = field[
+                    shifted_x[0:size, c * lanes : (c + 1) * lanes] = field[
                         r, plane, z : z + size, :
                     ]
                     for s in range(2):
                         low = 3 * lanes + (2 * c + s) * ch
-                        shifted_x[lo : lo + size, low : low + ch] = line[s, z : z + size, 0:ch]
+                        shifted_x[0:size, low : low + ch] = line[s, z : z + size, 0:ch]
                 acc[out * size : (out + 1) * size, :] += jnp.dot(
-                    shifted_x[lo : lo + size, :], weights[r % 2, a * per_a : (a + 1) * per_a, :],
+                    shifted_x[0:size, :], weights[r % 2, a * per_a : (a + 1) * per_a, :],
                     preferred_element_type=jnp.float32,
                 )
                 emit(r, out, norm)
@@ -372,14 +365,16 @@
         field[0, 1 + x, own : own + nz, :] = spread(t_in, x)
     send_rest(0)
     clear(line, shifted_x, weights, shifted_y)
-    clear(shifted.at[:, 0], shifted.at[:, nx + 1])
+    clear(shifted.at[0], shifted.at[nx + 1])
     loads[2].wait()
     build(0)
     conv(0)
     conv(1)
     squares = jnp.zeros((8, lanes), jnp.float32)
     for x in range(nx):
-        part = acc[x * ext + PAD : x * ext + PAD + nz, :].reshape(nz // 8, 8, lanes)
+        lo, size = rows_of(1)
+        z = x * size + PAD - lo
+        part = acc[z : z + nz, :].reshape(nz // 8, 8, lanes)
         squares = squares + jnp.sum(part * part, axis=0)
     start_sum(0, sums_x, sum(squares[:, j : j + 128] for j in range(0, lanes, 128)))
     conv(2)
@@ -424,7 +419,7 @@
             pltpu.VMEM((4, 3, 2, full, nx * ch), jnp.bfloat16),
             pltpu.VMEM((4, 2, 2, full * ch // 128, 128), jnp.bfloat16),
             pltpu.VMEM((2, full, 128), jnp.bfloat16),
-            pltpu.VMEM((3, nx + 2, ext, lanes), jnp.bfloat16),
+            pltpu.VMEM((nx + 2, ext, 3 * lanes), jnp.bfloat16),
             pltpu.VMEM((nx + 2, ext, lanes), jnp.bfloat16),
             pltpu.VMEM((ext, 4 * lanes), jnp.bfloat16),
             pltpu.VMEM((nx * ext, lanes), jnp.float32),

time: 35.6 us -> 35.5 us (level)
  no operation moved by 1% of the time
where the time goes in v6:
time: 35.5 us; the launch traced here: 35.3 us
  Pallas kernels  31.1 us (88%)
  between operations  2.34 us (7%)
  local copies, waits for them, and re-layouts  1.87 us (5%)
    pallas_call x1, Pallas kernels, on_device(): pl.pallas_call(functools.partial(kernel, counts), out_shape=(jax.ShapeDty...  31.1 us
    unnamed x1, local copies, waits for them, and re-layouts  1.87 us

profile of v6, /device:TPU:0, one launch (start us, length us, event | category | flops | bytes accessed | tf_op | source)
XLA Modules:
  0.0 35.3 jit_solution(7981469687573467195)
XLA Ops:
  0.6 31.1 %denoiser_step.1 = (f32[32,4,8,128]{3,2,1,0:T(8,128)}, f32[1,1]{1,0:T(1,128)}) custom-call(bf16[32,4,8,128]{3,2,1,0:T(8,128)(2,1)} %t_hbm.1, bf16[32,4,8,128]{3,2,1,0:T(8,128)(2,1)} %s_hbm.1, bf16[27,32,32]{2,1,0:T(8,128)(2,1)} %k1_hbm.1, bf16[27,32,32]{2,1,0:T(8,128)(2,1)} %k2_hbm.1), custom_call_target="tpu_custom_call" | custom-call | tf_op jit(solution)/shard_map/denoiser_step/pallas_call | solution.py:402
  31.7 1.9 %copy.8 = f32[32,4,8,128]{3,2,1,0:T(8,128)} copy(f32[32,4,8,128]{3,2,1,0:T(8,128)} %get-tuple-element.8) | data formatting | bytes 1048576

commit v7 on v6

--- a/solution.py
+++ b/solution.py
@@ -215,6 +215,7 @@
     def send_face(r, side):
         start, piece = span(r)
         x = nx - 1 if side else 0
+        send(r, lambda d: d == (2 * side - 1, 0, 0))
         for s in range(2):
             low = s * (ny - 1) * ch
             for q in range(parts):
@@ -222,7 +223,7 @@
                 edge_x[r, side, s, 0:piece, q * ch : (q + 1) * ch] = field[
                     r, 1 + x, z : z + piece, low : low + ch
                 ]
-        send(r, lambda d: d[0] == 2 * side - 1 and d[2] == 0)
+        send(r, lambda d: d[0] == 2 * side - 1 and d[1] != 0 and d[2] == 0)
 
     def send_rest(r):
         z, size = (own, nz) if r == 0 else (PAD, ext)
@@ -320,11 +321,23 @@
             def _():
                 emit(r, out, norm)
 
-        arrive(lambda d: d[0] != 0)
+        arrive(lambda d: d[0] != 0 and d[1] == 0)
         for side, plane, out, a in faces:
             @pl.when(inside((2 * side - 1, 0, 0), -1))
             def _():
                 x = nx - 1 if side else 0
+                base = a * per_a
+                for c in range(3):
+                    z = PAD - 1 + c + lo
+                    shifted_x[0:size, c * lanes : (c + 1) * lanes] = field[
+                        r, plane, z : z + size, :
+                    ]
+                acc[out * size : (out + 1) * size, :] += jnp.dot(
+                    shifted_x[0:size, 0 : 3 * lanes],
+                    weights[r % 2, base : base + 3 * lanes, :],
+                    preferred_element_type=jnp.float32,
+                )
+                arrive(lambda d: d[0] == 2 * side - 1 and d[1] != 0)
                 for s in range(2):
                     if r == 0:
                         for z in (PAD, own + nz):
@@ -338,14 +351,12 @@
                         ]
                 for c in range(3):
                     z = PAD - 1 + c + lo
-                    shifted_x[0:size, c * lanes : (c + 1) * lanes] = field[
-                        r, plane, z : z + size, :
-                    ]
                     for s in range(2):
                         low = 3 * lanes + (2 * c + s) * ch
                         shifted_x[0:size, low : low + ch] = line[s, z : z + size, 0:ch]
                 acc[out * size : (out + 1) * size, :] += jnp.dot(
-                    shifted_x[0:size, :], weights[r % 2, a * per_a : (a + 1) * per_a, :],
+                    shifted_x[0:size, 3 * lanes : per_a],
+                    weights[r % 2, base + 3 * lanes : base + per_a, :],
                     preferred_element_type=jnp.float32,
                 )
                 emit(r, out, norm)

time: 35.5 us -> 35.7 us (level)
  no operation moved by 1% of the time
where the time goes in v7:
time: 35.7 us; the launch traced here: 35.5 us
  Pallas kernels  31.2 us (87%)
  between operations  2.34 us (7%)
  local copies, waits for them, and re-layouts  1.87 us (5%)
    pallas_call x1, Pallas kernels, on_device(): pl.pallas_call(functools.partial(kernel, counts), out_shape=(jax.ShapeDty...  31.2 us
    unnamed x1, local copies, waits for them, and re-layouts  1.87 us

profile of v7, /device:TPU:0, one launch (start us, length us, event | category | flops | bytes accessed | tf_op | source)
XLA Modules:
  0.0 35.5 jit_solution(14459224097326031318)
XLA Ops:
  0.6 31.2 %denoiser_step.1 = (f32[32,4,8,128]{3,2,1,0:T(8,128)}, f32[1,1]{1,0:T(1,128)}) custom-call(bf16[32,4,8,128]{3,2,1,0:T(8,128)(2,1)} %t_hbm.1, bf16[32,4,8,128]{3,2,1,0:T(8,128)(2,1)} %s_hbm.1, bf16[27,32,32]{2,1,0:T(8,128)(2,1)} %k1_hbm.1, bf16[27,32,32]{2,1,0:T(8,128)(2,1)} %k2_hbm.1), custom_call_target="tpu_custom_call" | custom-call | tf_op jit(solution)/shard_map/denoiser_step/pallas_call | solution.py:413
  31.9 1.9 %copy.8 = f32[32,4,8,128]{3,2,1,0:T(8,128)} copy(f32[32,4,8,128]{3,2,1,0:T(8,128)} %get-tuple-element.8) | data formatting | bytes 1048576
